TPU v7x, 256 devices: a whole 4x4x8 slice. The times are simulated.
256 devices in a mesh: ctx: 32 (over z, x_hi, core), head: 8 (over y, x_lo).
Axes of the slice: x: 4 (x_hi: 2, x_lo: 2; x = x_hi * 2 + x_lo), y: 4, z: 8, core: 2. Of those that a mesh axis runs over, the one named last changes fastest.
Arguments:
- queries: float32 [512, 8, 2048], P('ctx', 'head'), may hold values from -80 to 80
- new_kv: float32 [2, 512, 8, 128], P(None, 'ctx', 'head'), may hold values from -24 to 24
- cache_keys: float32 [4, 32768, 8, 128], P(None, 'ctx', 'head'), may hold values from -4 to 4
- cache_values: float32 [4, 32768, 8, 128], P(None, 'ctx', 'head'), may hold values from -24 to 24
- new_lengths: int32 [4], replicated, may hold values from 1 to 192, 512 in all
- block_plan: int32 [128], P('ctx'), may hold values from 0 to 127, each once
Outputs:
- attended: float32 [512, 16384], P(('ctx', 'head'))
Inputs may be any that keep to these rules, and one draw needn't show every extreme that they name: `new_lengths`: the lengths sum to 512 and the largest is exactly 192. `block_plan`: every block number appears once.
All inputs are finite; a program needn't handle non-finite values.
Results may differ from a plain program's by a relative error of at most 0.0003.
Values sent between devices are 32-bit elements; how exact they have to be, the bound alone decides.
No kernel may reach another device: no remote copies, remote signals or barrier semaphores. Data moves between devices by JAX's collectives and lax.ppermute only.
A program may use at most 128 MiB of HBM per device.

v0:
```python
import jax
import jax.numpy as jnp
from jax import lax
from jax.sharding import PartitionSpec as P

REQS = 4


HIGHEST = lax.Precision.HIGHEST
NEG_FLOOR = -1e30
QUERY_BLOCK = 32


def partial_scores(query_rows, keys, values, allowed):
    scores = jnp.dot(
        query_rows, keys.T, precision=HIGHEST, preferred_element_type=jnp.float32
    ) * keys.shape[1] ** (-0.5)
    scores = jnp.where(allowed, scores, NEG_FLOOR)
    peak = jnp.max(scores, axis=1)
    weights = jnp.where(allowed, jnp.exp(scores - peak[:, None]), 0.0)
    total = jnp.sum(weights, axis=1)
    summed = jnp.dot(weights, values, precision=HIGHEST, preferred_element_type=jnp.float32)
    return (peak, total, summed)


def make_step(chosen, keys, values, base, span):

    def cache_block(index, state):
        offset = index * span
        rows_here = lax.dynamic_slice_in_dim(chosen, offset, span, 0)
        peak, mass, summed = partial_scores(rows_here, keys, values, True)
        where = base + offset
        return (
            lax.dynamic_update_slice_in_dim(state[0], peak, where, 0),
            lax.dynamic_update_slice_in_dim(state[1], mass, where, 0),
            lax.dynamic_update_slice_in_dim(state[2], summed, where, 0),
        )

    return cache_block


def body(queries, new_kv, cache_keys, cache_values, new_lengths, block_plan):
    tok_dev = queries.shape[0]
    width = queries.shape[2]
    head_dim = new_kv.shape[3]
    heads = width // head_dim
    n_ctx = lax.axis_size("ctx")
    n_head = lax.axis_size("head")
    me = lax.axis_index("ctx")
    gathered_q, gathered_kv, gathered_plan = (
        lax.all_gather(queries, "ctx", axis=0, tiled=True),
        lax.all_gather(new_kv, "ctx", axis=1, tiled=True),
        lax.all_gather(block_plan, "ctx", axis=0, tiled=True),
    )
    total = gathered_q.shape[0]
    nblocks = gathered_plan.shape[0]
    block = total // nblocks
    most = 3 * total // (2 * REQS)
    slots = -(-most // QUERY_BLOCK) * QUERY_BLOCK
    rows = jnp.arange(total, dtype=jnp.int32)
    packed = jnp.repeat(gathered_plan, block) * block + rows % block
    ends = jnp.cumsum(new_lengths)
    starts = ends - new_lengths
    request = jnp.sum((packed[:, None] >= ends[None, :]).astype(jnp.int32), axis=1)
    chat_ids = jnp.arange(REQS, dtype=jnp.int32)
    onehot = (request[:, None] == chat_ids[None, :]).astype(jnp.int32)
    position = packed - jnp.sum(onehot * starts[None, :], axis=1)
    block_ids = jnp.arange(nblocks, dtype=jnp.int32)
    placed = jnp.sum(
        (gathered_plan[None, :] == block_ids[:, None]).astype(jnp.int32) * block_ids[None, :],
        axis=1,
    )
    span = QUERY_BLOCK * heads
    offsets = jnp.arange(slots, dtype=jnp.int32)
    state = (
        jnp.full((REQS * slots * heads,), NEG_FLOOR, jnp.float32),
        jnp.zeros((REQS * slots * heads,), jnp.float32),
        jnp.zeros((REQS * slots * heads, head_dim), jnp.float32),
    )
    for chat in range(REQS):
        wanted = jnp.minimum(starts[chat] + offsets, total - 1)
        source_rows = placed[wanted // block] * block + wanted % block
        chosen = gathered_q[source_rows, 0].reshape(slots * heads, head_dim)
        cache_block = make_step(
            chosen, cache_keys[chat, :, 0], cache_values[chat, :, 0], chat * slots * heads, span
        )
        live_blocks = (new_lengths[chat] + QUERY_BLOCK - 1) // QUERY_BLOCK
        state = lax.fori_loop(0, live_blocks, cache_block, state)
    slot_index = request * slots + position
    peak_rows = state[0].reshape(REQS * slots, heads)[slot_index]
    mass_rows = state[1].reshape(REQS * slots, heads)[slot_index]
    sum_rows = state[2].reshape(REQS * slots, width)[slot_index]
    own_start = me * tok_dev
    own_request = lax.dynamic_slice_in_dim(request, own_start, tok_dev, 0)
    own_position = lax.dynamic_slice_in_dim(position, own_start, tok_dev, 0)
    allowed = (own_request[:, None] == request[None, :]) & (
        position[None, :] <= own_position[:, None]
    )
    allowed = jnp.repeat(allowed, heads, axis=0)
    fresh_peak, fresh_mass, fresh_sum = partial_scores(
        queries[:, 0].reshape(tok_dev * heads, head_dim),
        gathered_kv[0, :, 0],
        gathered_kv[1, :, 0],
        allowed,
    )
    fresh_peak = fresh_peak.reshape(tok_dev, heads)
    fresh_mass = fresh_mass.reshape(tok_dev, heads)
    fresh_sum = fresh_sum.reshape(tok_dev, heads, head_dim)
    home_sum, home_peak, home_mass = (
        lax.all_to_all(
            sum_rows.reshape(n_ctx, tok_dev, width), "ctx", split_axis=0, concat_axis=0, tiled=True
        ),
        lax.all_to_all(
            peak_rows.reshape(n_ctx, tok_dev, heads), "ctx", split_axis=0, concat_axis=0, tiled=True
        ),
        lax.all_to_all(
            mass_rows.reshape(n_ctx, tok_dev, heads), "ctx", split_axis=0, concat_axis=0, tiled=True
        ),
    )
    top = jnp.maximum(fresh_peak, jnp.max(home_peak, axis=0))
    fresh_scale = jnp.exp(fresh_peak - top)
    home_scale = jnp.exp(home_peak - top[None])
    mass = fresh_mass * fresh_scale + jnp.sum(home_mass * home_scale, axis=0)
    summed = fresh_sum * fresh_scale[:, :, None] + jnp.sum(
        home_sum.reshape(n_ctx, tok_dev, heads, head_dim) * home_scale[:, :, :, None], axis=0
    )
    merged = (summed / mass[:, :, None]).reshape(tok_dev, width)
    arranged = merged.reshape(n_head, tok_dev // n_head, 1, width)
    regrouped = lax.all_to_all(arranged, "head", split_axis=0, concat_axis=2, tiled=True)
    return regrouped.reshape(tok_dev // n_head, n_head * width)


def solution(mesh):
    placed = (
        P("ctx", "head", None),
        P(None, "ctx", "head", None),
        P(None, "ctx", "head", None),
        P(None, "ctx", "head", None),
        P(),
        P("ctx"),
    )
    return jax.shard_map(
        body, mesh=mesh, in_specs=placed, out_specs=P(("ctx", "head"), None), check_vma=False
    )
```

profile of v0, /device:TPU:4, one launch (start us, length us, event | category | flops | bytes accessed | tf_op | source)
XLA Modules:
  0.0 469.0 jit_solution(13527624679056816162)
XLA Ops:
  7.3 1.5 fusion.60
  14.2 20.2 %all-reduce.4 = s32[128]{0:T(128)S(1)} all-reduce(s32[128]{0:T(128)S(1)} %dynamic-update-slice), channel_id=1, replica_groups=mesh['ctx'=32,'head'=8] {'ctx'}, use_global_device_ids=true, to_apply=%add.4 | all-reduce | flops 128 | bytes 1024
  37.7 1.6 gather_fusion
  39.9 1.6 gather_fusion.2
  42.1 1.6 gather_fusion.4
  44.4 1.6 gather_fusion.6
  48.8 3.9 slice_bitcast_fusion
  52.7 44.9 %all-gather.2.cloned.1.call-done = f32[512,1,2048]{2,1,0:T(1,128)} async-done(((f32[16,1,2048]{2,1,0:T(1,128)}), f32[512,1,2048]{2,1,0:T(1,128)}) %all-gather.2.cloned.1.call-update) | async-done | bytes 4194320 | tf_op jit(solution)/shard_map/all_gather | solution.py:51
  97.6 3.7 gather_fusion.1
  102.7 2.9 broadcast_in_dim.35
  105.6 31.5 %while.62 = (s32[]{:T(128)}, f32[12288]{0:T(1024)S(1)}, f32[12288]{0:T(1024)S(1)}, f32[12288,128]{1,0:T(8,128)}, s32[]{:T(128)}, /*index=5*/f32[3072,128]{1,0:T(...) while((s32[]{:T(128)}, f32[12288]{0:T(1024)S(1)}, ...), condition=%wide.region_8.9_spmd, body=%wide.region_5.8_spmd.sunk | while | flops 1614281728 | bytes 7880916 | solution.py:88
  105.6 3.1 multiply_reduce_fusion.10
  108.7 3.7 fusion.91
  113.4 3.1 multiply_reduce_fusion.10
  116.5 3.7 fusion.91
  121.3 3.1 multiply_reduce_fusion.10
  124.3 3.7 fusion.91
  129.1 3.1 multiply_reduce_fusion.10
  132.2 3.7 fusion.91
  137.1 3.7 gather_fusion.3
  142.2 47.1 %while.63 = (s32[]{:T(128)}, f32[12288]{0:T(1024)S(1)}, f32[12288]{0:T(1024)S(1)}, f32[12288,128]{1,0:T(8,128)}, s32[]{:T(128)}, /*index=5*/f32[3072,128]{1,0:T(...) while((s32[]{:T(128)}, f32[12288]{0:T(1024)S(1)}, ...), condition=%wide.region_12.13_spmd, body=%wide.region_9.12_spmd.sunk | while | flops 1614281728 | bytes 7880925 | solution.py:88
  142.2 3.1 multiply_reduce_fusion.11
  145.3 3.7 fusion.95
  150.0 3.1 multiply_reduce_fusion.11
  153.1 3.7 fusion.95
  157.9 3.1 multiply_reduce_fusion.11
  161.0 3.8 fusion.95
  165.8 3.1 multiply_reduce_fusion.11
  168.8 3.7 fusion.95
  173.6 3.1 multiply_reduce_fusion.11
  176.7 3.7 fusion.95
  181.4 3.1 multiply_reduce_fusion.11
  184.5 3.7 fusion.95
  189.3 4.9 %gather_fusion.5 = f32[192,2048]{1,0:T(8,128)S(1)} fusion(f32[512,1,2048]{2,1,0:T(1,128)} %all-gather.2.cloned.1.call-done, s32[192]{0:T(256)S(1)} %bitcast.108), kind=kCustom, calls=%fused_computation.5 | custom fusion | bytes 3147264 | tf_op jit(solution)/shard_map/gather | solution.py:83
  195.6 23.7 %while.64 = (s32[]{:T(128)}, f32[12288]{0:T(1024)S(1)}, f32[12288]{0:T(1024)S(1)}, f32[12288,128]{1,0:T(8,128)}, s32[]{:T(128)}, /*index=5*/f32[3072,128]{1,0:T(...) while((s32[]{:T(128)}, f32[12288]{0:T(1024)S(1)}, ...), condition=%wide.region_16.17_spmd, body=%wide.region_13.16_spmd.sunk | while | flops 1614281728 | bytes 7880945 | solution.py:88
  195.8 3.1 multiply_reduce_fusion.12
  198.8 3.8 fusion.99
  203.6 3.1 multiply_reduce_fusion.12
  206.7 3.7 fusion.99
  211.5 3.1 multiply_reduce_fusion.12
  214.5 3.7 fusion.99
  219.3 5.4 %gather_fusion.7 = f32[192,2048]{1,0:T(8,128)S(1)} fusion(f32[512,1,2048]{2,1,0:T(1,128)} %all-gather.2.cloned.1.call-done, s32[192]{0:T(256)S(1)} %bitcast.107), kind=kCustom, calls=%fused_computation.7 | custom fusion | bytes 3147264 | tf_op jit(solution)/shard_map/gather | solution.py:83
  226.1 33.3 %while.65 = (s32[]{:T(128)}, f32[12288]{0:T(1024)S(1)}, f32[12288]{0:T(1024)S(1)}, f32[12288,128]{1,0:T(8,128)}, s32[]{:T(128)}, /*index=5*/f32[3072,128]{1,0:T(...) while((s32[]{:T(128)}, f32[12288]{0:T(1024)S(1)}, ...), condition=%wide.region_20.21_spmd, body=%wide.region_17.20_spmd.sunk | while | flops 1614281728 | bytes 7880945 | solution.py:88
  226.3 2.9 multiply_reduce_fusion.13
  229.2 2.7 fusion.103
  233.0 2.9 multiply_reduce_fusion.13
  235.8 2.7 fusion.103
  239.6 2.9 multiply_reduce_fusion.13
  242.5 2.7 fusion.103
  246.2 2.9 multiply_reduce_fusion.13
  249.1 2.7 fusion.103
  252.9 2.9 multiply_reduce_fusion.13
  255.8 2.7 fusion.103
  261.4 7.2 %all-to-all-start = ((f32[32,1,256]{2,1,0:T(1,128)}), f32[32,1,256]{2,1,0:T(1,128)S(1)}, u32[]{:S(2)}, u32[]{:S(2)}) async-start(f32[32,1,256]{2,1,0:T(1,128)} %reshape.738), calls=%async_computation | async-start | bytes 65536 | tf_op jit(solution)/shard_map/all_to_all | solution.py:113
  270.6 5.4 %all-to-all-done = f32[32,1,256]{2,1,0:T(1,128)S(1)} async-done(((f32[32,1,256]{2,1,0:T(1,128)}), f32[32,1,256]{2,1,0:T(1,128)S(1)}, u32[]{:S(2)}, u32[]{:S(2)}) %all-to-all-start) | async-done | bytes 32800 | tf_op jit(solution)/shard_map/all_to_all | solution.py:113
  276.0 6.2 %all-to-all-start.2 = ((f32[32,1,256]{2,1,0:T(1,128)}), f32[32,1,256]{2,1,0:T(1,128)S(1)}, u32[]{:S(2)}, u32[]{:S(2)}) async-start(f32[32,1,256]{2,1,0:T(1,128)} %reshape.740), calls=%async_computation.2 | async-start | bytes 65536 | tf_op jit(solution)/shard_map/all_to_all | solution.py:116
  282.2 7.1 %reshape.646 = f32[768,2048]{1,0:T(8,128)} reshape(f32[12288,128]{1,0:T(8,128)} %get-tuple-element.378) | data formatting | bytes 12582912 | tf_op jit(solution)/shard_map/reshape | solution.py:92
  289.2 8.2 %gather_fusion.9 = f32[512,2048]{1,0:T(8,128)} fusion(f32[768,2048]{1,0:T(8,128)} %reshape.646, s32[1024]{0:T(1024)S(1)} %pad_clamp_fusion), kind=kCustom, calls=%fused_computation.9 | custom fusion | bytes 8390656 | tf_op jit(solution)/shard_map/gather | solution.py:92
  297.4 10.1 %all-to-all-start.1 = ((f32[32,16,2048]{2,1,0:T(8,128)}), f32[32,16,2048]{2,1,0:T(8,128)}, u32[]{:S(2)}, u32[]{:S(2)}) async-start(f32[32,16,2048]{2,1,0:T(8,128)} %bitcast.106), calls=%async_computation.1 | async-start | bytes 8388608 | tf_op jit(solution)/shard_map/all_to_all | solution.py:110
  307.7 125.3 %all_gather.10 = f32[2,512,1,128]{3,1,2,0:T(8,128)S(1)} all-gather(f32[2,16,1,128]{3,1,2,0:T(8,128)S(1)} %bitcast.123), channel_id=1, replica_groups=mesh['ctx'=32,'head'=8] {'ctx'}, dimensions={1}, use_global_device_ids=true | all-gather | bytes 540672 | tf_op jit(solution)/shard_map/all_gather | solution.py:52
  436.6 2.6 mul.222
  439.2 4.9 %mul.223 = f32[32,16,2048]{2,1,0:T(8,128)} reshape(f32[32,16,16,128]{3,2,1,0:T(8,128)} %mul.222) | data formatting | bytes 8388608 | tf_op jit(solution)/shard_map/mul | solution.py:125
  444.1 3.9 multiply_reduce_fusion.4
  448.7 12.3 %all_to_all.30 = f32[8,2,1,2048]{3,1,2,0:T(2,128)S(1)} all-to-all(f32[8,2,1,2048]{3,1,2,0:T(2,128)S(1)} %bitcast.119), channel_id=1, replica_groups=mesh['ctx'=32,'head'=8] {'head'}, dimensions={0} | all-to-all | bytes 262144 | tf_op jit(solution)/shard_map/all_to_all | solution.py:129
  (129 shorter events, 43.8 us)
Async XLA Ops:
  6.5 91.1 %all-gather.2.cloned.1.call-start = ((), (), s32[]{:S(2)}) async-start(), calls=%async_computation.4 | async-start | bytes 4325376 | tf_op jit(solution)/shard_map/all_gather | solution.py:51
  261.4 14.6 %all-to-all-start = ((f32[32,1,256]{2,1,0:T(1,128)}), f32[32,1,256]{2,1,0:T(1,128)S(1)}, u32[]{:S(2)}, u32[]{:S(2)}) async-start(f32[32,1,256]{2,1,0:T(1,128)} %reshape.738), calls=%async_computation | async-start | bytes 65536 | tf_op jit(solution)/shard_map/all_to_all | solution.py:113
  276.0 21.4 %all-to-all-start.2 = ((f32[32,1,256]{2,1,0:T(1,128)}), f32[32,1,256]{2,1,0:T(1,128)S(1)}, u32[]{:S(2)}, u32[]{:S(2)}) async-start(f32[32,1,256]{2,1,0:T(1,128)} %reshape.740), calls=%async_computation.2 | async-start | bytes 65536 | tf_op jit(solution)/shard_map/all_to_all | solution.py:116
  297.4 10.3 %copy-start.1 = (f32[2,16,1,128]{3,2,1,0:T(1,128)S(1)}, f32[2,16,1,128]{3,2,1,0:T(1,128)}, u32[]{:S(2)}) copy-start(f32[2,16,1,128]{3,2,1,0:T(1,128)} %param.15) | copy-start | bytes 49156
  297.4 135.7 %copy-start = (f32[16,1,2048]{2,1,0:T(1,128)S(1)}, f32[16,1,2048]{2,1,0:T(1,128)}, u32[]{:S(2)}) copy-start(f32[16,1,2048]{2,1,0:T(1,128)} %param.14) | copy-start | bytes 393220
  297.4 146.7 %all-to-all-start.1 = ((f32[32,16,2048]{2,1,0:T(8,128)}), f32[32,16,2048]{2,1,0:T(8,128)}, u32[]{:S(2)}, u32[]{:S(2)}) async-start(f32[32,16,2048]{2,1,0:T(8,128)} %bitcast.106), calls=%async_computation.1 | async-start | bytes 8388608 | tf_op jit(solution)/shard_map/all_to_all | solution.py:110
Sparse Core Ops, SparseCore 0:
  10.1 87.4 all-gather.1
where the time goes:
time: 478 us; the launch traced here: 469 us
  blocking collectives  158 us (33%)
  matrix products  118 us (25%)
  local copies, waits for them, and re-layouts  78.8 us (16%)
  waiting for transfers between devices  51 us (11%)
  starting transfers between devices  23.5 us (5%)
  other arithmetic  21.8 us (5%)
  between operations  17.6 us (4%)
    all_gather x1, blocking collectives, body(): lax.all_gather(new_kv, 'ctx', axis=1, tiled=True)  125 us
    dot_general x19, matrix products, partial_scores(): jnp.dot(weights, values, precision=HIGHEST, preferred_element_type=jnp.fl...  62.7 us
    dot_general x19, matrix products, partial_scores(): jnp.dot(query_rows, keys.T, precision=HIGHEST, preferred_element_type=jnp...  55 us
    all_gather x1, waiting for transfers between devices, body(): lax.all_gather(queries, 'ctx', axis=0, tiled=True)  44.9 us
    unnamed x1, blocking collectives  20.2 us
    gather x4, local copies, waits for them, and re-layouts, body(): chosen = gathered_q[source_rows, 0].reshape(slots * heads, head_dim)  17.8 us
    all_to_all x1, blocking collectives, body(): lax.all_to_all(arranged, 'head', split_axis=0, concat_axis=2, tiled=True)  12.3 us
    all_to_all x1, starting transfers between devices, body(): lax.all_to_all(sum_rows.reshape(n_ctx, tok_dev, width), 'ctx', split_axis...  10.1 us
  transfers between devices with their start and end apart: 4, of which 2 were waited for; matrix products, arithmetic and copies ran while one was open for 11% of the time, Pallas kernels for 0%

commit v1 on v0

v1 whole, which is shorter than its diff:
```python
import functools
import math

import jax
import jax.numpy as jnp
from jax import lax
from jax.experimental import pallas as pl
from jax.experimental.pallas import tpu as pltpu
from jax.sharding import PartitionSpec as P

REQS = 4
HD = 128
HEADS = 8
TOK = 16
BLOCK = 4
TOTAL = 512
NBLOCKS = TOTAL // BLOCK
TILE = 32
COLS = TILE * HEADS
POSITIONS = 2048
CHUNK = 512
CHUNKS = POSITIONS // CHUNK
FRESH = 2 * TOK
SLOTS = 16
SLOT_TOK = TOTAL // SLOTS
MAX_TILES = TOTAL // TILE + REQS
NEG = -1e30
SCALE = HD ** (-0.5) * math.log2(math.e)
NT = (((1,), (1,)), ((), ()))
OFFSETS = (0, -1, 1, -2, 2, -3, 3)


def split(x):
    high = x.astype(jnp.bfloat16)
    low = (x - high.astype(jnp.float32)).astype(jnp.bfloat16)
    return high, low


def prepare_kernel(own_k, other_k, own_v, other_v, keys, values):
    half = POSITIONS // 2
    for place, (k, v) in enumerate(((own_k, own_v), (other_k, other_v))):
        rows = pl.ds(place * half, half)
        high, low = split(k[0])
        keys[0, rows, 0:HD] = high
        keys[0, rows, HD : 2 * HD] = high
        keys[0, rows, 2 * HD : 3 * HD] = low
        high, low = split(v[0].T)
        values[0, 0:HD, rows] = high
        values[0, HD : 2 * HD, rows] = low


def prepare(own_k, other_k, own_v, other_v):
    half = POSITIONS // 2
    source = pl.BlockSpec((1, half, HD), lambda r: (r, 0, 0))
    return pl.pallas_call(
        prepare_kernel,
        grid=(REQS,),
        in_specs=[source] * 4,
        out_specs=[
            pl.BlockSpec((1, POSITIONS, 3 * HD), lambda r: (r, 0, 0)),
            pl.BlockSpec((1, 2 * HD, POSITIONS), lambda r: (r, 0, 0)),
        ],
        out_shape=[
            jax.ShapeDtypeStruct((REQS, POSITIONS, 3 * HD), jnp.bfloat16),
            jax.ShapeDtypeStruct((REQS, 2 * HD, POSITIONS), jnp.bfloat16),
        ],
        compiler_params=pltpu.CompilerParams(vmem_limit_bytes=40 << 20),
        cost_estimate=pl.CostEstimate(flops=10**7, bytes_accessed=16 << 20, transcendentals=0),
        name="prepare",
    )(own_k, other_k, own_v, other_v)


def attend_kernel(
    lengths, plan, place, *refs
):
    pieces, refs = refs[:9], refs[9:]
    fresh_own, fresh_other, keys_hbm, values_hbm, out = refs[:5]
    (
        queries, keys, values, fresh_keys, fresh_values, fresh_packed,
        weights, rows, scores_a, scores_b, new_a, new_b, peak_a, peak_b,
        placed, tile_req, tile_first, tile_start, tile_last, sems, kv_sems,
    ) = refs[5:]
    me = place[0]
    z = me // 4
    corner = lax.rem(me, 4)

    copies = []
    for index, piece in enumerate(pieces):
        offset = OFFSETS[index] if index < 7 else 4
        source_z = lax.rem(z + offset + 8, 8)
        for part in range(piece.shape[0] // TOK):
            which = part + (2 if index == 8 else 0)
            target = source_z * 4 + jnp.bitwise_xor(which, corner)
            copies.append(
                pltpu.make_async_copy(
                    piece.at[pl.ds(part * TOK, TOK)],
                    queries.at[pl.ds(target * TOK, TOK)],
                    sems.at[len(copies)],
                )
            )
    for copy in copies:
        copy.start()

    def kv_copies(req):
        return (
            pltpu.make_async_copy(keys_hbm.at[req], keys.at[req], kv_sems.at[req, 0]),
            pltpu.make_async_copy(values_hbm.at[req], values.at[req], kv_sems.at[req, 1]),
        )

    for req in range(REQS):
        for copy in kv_copies(req):
            copy.start()

    def place_block(j, _):
        placed[plan[j]] = j
        return 0

    lax.fori_loop(0, NBLOCKS, place_block, 0)

    begin = jnp.int32(0)
    tiles = jnp.int32(0)
    for req in range(REQS):
        end = begin + lengths[req]
        count = (lengths[req] + TILE - 1) // TILE

        def list_tile(t, _, req=req, begin=begin, end=end, tiles=tiles):
            tile_req[tiles + t] = req
            tile_first[tiles + t] = begin
            tile_start[tiles + t] = begin + t * TILE
            tile_last[tiles + t] = end - 1
            return 0

        lax.fori_loop(0, count, list_tile, 0)
        begin = end
        tiles = tiles + count

    for half, fresh in enumerate((fresh_own, fresh_other)):
        span = pl.ds(half * TOK, TOK)
        high, low = split(fresh[0])
        fresh_keys[span, 0:HD] = high
        fresh_keys[span, HD : 2 * HD] = high
        fresh_keys[span, 2 * HD : 3 * HD] = low
        holder = jnp.bitwise_xor(me, half)
        for u in range(TOK):
            number = plan[holder * (TOK // BLOCK) + u // BLOCK] * BLOCK + u % BLOCK
            fresh_packed[half * TOK + u : half * TOK + u + 1, :] = jnp.full((1, COLS), number, jnp.int32)
    high, low = split(jnp.concatenate([fresh_own[1], fresh_other[1]], axis=0).T)
    fresh_values[0:HD] = high
    fresh_values[HD : 2 * HD] = low

    out[...] = jnp.zeros_like(out)
    for copy in copies:
        copy.wait()

    lane = lax.broadcasted_iota(jnp.int32, (1, COLS), 1) // HEADS
    lanes = lax.broadcasted_iota(jnp.int32, (HEADS, HD), 1)

    def row_of(index, t):
        packed = jnp.minimum(tile_start[index] + t, tile_last[index])
        return placed[packed // BLOCK] * BLOCK + lax.rem(packed, BLOCK)

    def load(index):
        for t in range(TILE):
            rows[pl.ds(t * HEADS, HEADS), :] = queries[row_of(index, t)]
        high, low = split(rows[...] * SCALE)
        weights[:, 0:HD] = high
        weights[:, HD : 2 * HD] = low
        weights[:, 2 * HD : 3 * HD] = high

    def arrive(index):
        req = tile_req[index]

        @pl.when(tile_start[index] == tile_first[index])
        def _():
            for copy in kv_copies(req):
                copy.wait()

    def score_chunk(index, c, scores, peak):
        part = lax.dot_general(
            keys[tile_req[index], pl.ds(c * CHUNK, CHUNK), :], weights[...], NT,
            preferred_element_type=jnp.float32,
        )
        scores[pl.ds(c * CHUNK, CHUNK), :] = part
        top = jnp.max(part.reshape(CHUNK // 8, 8, COLS), axis=0)
        return top if peak is None else jnp.maximum(peak, top)

    def score_fresh(index, new, peak):
        part = lax.dot_general(
            fresh_keys[...], weights[...], NT, preferred_element_type=jnp.float32
        )
        number = fresh_packed[...]
        latest = jnp.minimum(tile_start[index] + lane, tile_last[index])
        allowed = (number >= tile_first[index]) & (number <= latest)
        part = jnp.where(allowed, part, NEG)
        new[...] = part
        return jnp.maximum(peak, jnp.max(part.reshape(FRESH // 8, 8, COLS), axis=0))

    def weigh(part, top):
        p = jnp.exp2(part - top)
        high, low = split(p)
        return jnp.sum(p.reshape(part.shape[0] // 8, 8, COLS), axis=0), high, low

    def accumulate(value, high, low, acc):
        first = jnp.dot(value, high, preferred_element_type=jnp.float32)
        second = jnp.dot(value[0:HD], low, preferred_element_type=jnp.float32)
        both = first[0:HD] + first[HD : 2 * HD] + second
        return both if acc is None else acc + both

    def finish(index, top, mass, acc):
        total = jnp.sum(mass, axis=0, keepdims=True)
        done = (acc / total).T
        level = jnp.broadcast_to(top + jnp.log2(total), (HD, COLS)).T
        for t in range(TILE):
            row = row_of(index, t)
            slot = row // SLOT_TOK
            inside = lax.rem(row, SLOT_TOK)
            out[slot, inside] = done[t * HEADS : (t + 1) * HEADS]
            out[slot, SLOT_TOK] = jnp.where(
                lanes == inside, level[t * HEADS : (t + 1) * HEADS], out[slot, SLOT_TOK]
            )

    def step(now, later, scores_now, new_now, peak_now, scores_later, new_later, peak_later):
        load(later)
        top = jnp.max(peak_now[...], axis=0, keepdims=True)
        mass, high, low = weigh(new_now[...], top)
        acc = accumulate(fresh_values[...], high, low, None)
        peak = None
        for c in range(CHUNKS):
            peak = score_chunk(later, c, scores_later, peak)
            more, high, low = weigh(scores_now[pl.ds(c * CHUNK, CHUNK), :], top)
            mass = mass + more
            acc = accumulate(
                values[tile_req[now], :, pl.ds(c * CHUNK, CHUNK)], high, low, acc
            )
        peak_later[...] = score_fresh(later, new_later, peak)
        finish(now, top, mass, acc)

    arrive(0)
    load(0)
    peak = None
    for c in range(CHUNKS):
        peak = score_chunk(0, c, scores_a, peak)
    peak_a[...] = score_fresh(0, new_a, peak)

    def pair(j, _):
        now = 2 * j
        for this, (a, b) in enumerate(
            (
                ((scores_a, new_a, peak_a), (scores_b, new_b, peak_b)),
                ((scores_b, new_b, peak_b), (scores_a, new_a, peak_a)),
            )
        ):
            current = now + this
            following = jnp.minimum(current + 1, tiles - 1)

            @pl.when(current < tiles)
            def _():
                @pl.when(current + 1 < tiles)
                def _():
                    arrive(following)

                step(current, following, *a, *b)

        return 0

    lax.fori_loop(0, (tiles + 1) // 2, pair, 0)


def attend(lengths, plan, place, pieces, fresh_own, fresh_other, keys, values):
    smem = pl.BlockSpec(memory_space=pltpu.SMEM)
    vmem = pl.BlockSpec(memory_space=pltpu.VMEM)
    hbm = pl.BlockSpec(memory_space=pl.ANY)
    return pl.pallas_call(
        attend_kernel,
        in_specs=[smem] * 3 + [hbm] * 9 + [vmem] * 2 + [hbm] * 2,
        out_specs=vmem,
        out_shape=jax.ShapeDtypeStruct((SLOTS, SLOT_TOK + 1, HEADS, HD), jnp.float32),
        scratch_shapes=[
            pltpu.VMEM((TOTAL, HEADS, HD), jnp.float32),
            pltpu.VMEM((REQS, POSITIONS, 3 * HD), jnp.bfloat16),
            pltpu.VMEM((REQS, 2 * HD, POSITIONS), jnp.bfloat16),
            pltpu.VMEM((FRESH, 3 * HD), jnp.bfloat16),
            pltpu.VMEM((2 * HD, FRESH), jnp.bfloat16),
            pltpu.VMEM((FRESH, COLS), jnp.int32),
            pltpu.VMEM((COLS, 3 * HD), jnp.bfloat16),
            pltpu.VMEM((COLS, HD), jnp.float32),
            pltpu.VMEM((POSITIONS, COLS), jnp.float32),
            pltpu.VMEM((POSITIONS, COLS), jnp.float32),
            pltpu.VMEM((FRESH, COLS), jnp.float32),
            pltpu.VMEM((FRESH, COLS), jnp.float32),
            pltpu.VMEM((8, COLS), jnp.float32),
            pltpu.VMEM((8, COLS), jnp.float32),
            pltpu.SMEM((NBLOCKS,), jnp.int32),
            pltpu.SMEM((MAX_TILES,), jnp.int32),
            pltpu.SMEM((MAX_TILES,), jnp.int32),
            pltpu.SMEM((MAX_TILES,), jnp.int32),
            pltpu.SMEM((MAX_TILES,), jnp.int32),
            pltpu.SemaphoreType.DMA((32,)),
            pltpu.SemaphoreType.DMA((REQS, 2)),
        ],
        compiler_params=pltpu.CompilerParams(vmem_limit_bytes=48 << 20),
        cost_estimate=pl.CostEstimate(
            flops=34 * 10**9, bytes_accessed=14 << 20, transcendentals=10**7
        ),
        name="attend",
    )(lengths, plan, place, *pieces, fresh_own, fresh_other, keys, values)


def merge_kernel(parts, out):
    level = parts[:, SLOT_TOK]
    top = jnp.max(level, axis=0)
    share = jnp.exp2(level - top[None])
    share = share / jnp.sum(share, axis=0)[None]
    for t in range(SLOT_TOK):
        acc = parts[0, t] * share[0][:, t : t + 1]
        for c in range(1, SLOTS):
            acc = acc + parts[c, t] * share[c][:, t : t + 1]
        out[t] = acc


def merge(parts):
    return pl.pallas_call(
        merge_kernel,
        out_shape=jax.ShapeDtypeStruct((SLOT_TOK, HEADS, HD), jnp.float32),
        compiler_params=pltpu.CompilerParams(vmem_limit_bytes=24 << 20),
        name="merge",
    )(parts)


def body(queries, new_kv, cache_keys, cache_values, new_lengths, block_plan):
    me = lax.axis_index("ctx")
    core = me % 2
    n_ctx = 32
    n_head = 8

    def send(x, target):
        return lax.ppermute(x, "ctx", [(i, target(i)) for i in range(n_ctx)])

    def across(i):
        return i ^ 1

    def up(i):
        return (i + 4) % n_ctx

    def down(i):
        return (i - 4) % n_ctx

    q = queries.reshape(TOK, 2, HEADS, HD)
    mine = lax.dynamic_index_in_dim(q, core, 1, keepdims=False)
    theirs = lax.dynamic_index_in_dim(q, 1 - core, 1, keepdims=False)
    own = jnp.concatenate(
        [mine, send(theirs, across), send(mine, lambda i: i ^ 2), send(theirs, lambda i: i ^ 3)],
        axis=0,
    )
    plan = lax.all_to_all(
        jnp.broadcast_to(block_plan[None], (n_ctx,) + block_plan.shape),
        "ctx", split_axis=0, concat_axis=0, tiled=True,
    ).reshape(NBLOCKS)
    keys, values = prepare(
        cache_keys[:, :, 0], send(cache_keys, across)[:, :, 0],
        cache_values[:, :, 0], send(cache_values, across)[:, :, 0],
    )
    fresh = new_kv[:, :, 0]
    fresh_other = send(fresh, across)
    rising, falling = [own], [own]
    for _ in range(3):
        rising.append(send(rising[-1], up))
        falling.append(send(falling[-1], down))
    pieces = [own]
    for k in range(1, 4):
        pieces += [rising[k], falling[k]]
    pieces += [send(rising[3][: 2 * TOK], up), send(falling[3][2 * TOK :], down)]
    parts = attend(new_lengths, plan, me.reshape(1), pieces, fresh, fresh_other, keys, values)
    groups = [[i for i in range(n_ctx) if i % 2 == c] for c in range(2)]
    home = lax.all_to_all(
        parts, "ctx", split_axis=0, concat_axis=0, tiled=True, axis_index_groups=groups
    )
    merged = merge(home).reshape(2, TOK, HEADS, HD)
    keep = lax.dynamic_index_in_dim(merged, core, 0, keepdims=False)
    give = lax.dynamic_index_in_dim(merged, 1 - core, 0, keepdims=False)
    got = send(give, across)
    first = jnp.where(core == 0, keep, got)
    second = jnp.where(core == 0, got, keep)
    wide = jnp.concatenate([first, second], axis=1).reshape(n_head, TOK // n_head, 1, 2 * HEADS * HD)
    regrouped = lax.all_to_all(wide, "head", split_axis=0, concat_axis=2, tiled=True)
    return regrouped.reshape(TOK // n_head, n_head * 2 * HEADS * HD)


def solution(mesh):
    placed = (
        P("ctx", "head", None),
        P(None, "ctx", "head", None),
        P(None, "ctx", "head", None),
        P(None, "ctx", "head", None),
        P(),
        P("ctx"),
    )
    return jax.shard_map(
        body, mesh=mesh, in_specs=placed, out_specs=P(("ctx", "head"), None), check_vma=False
    )
```

time: 478 us -> 183 us (0.38); the launches traced: 469 us -> 181 us
  matrix products: 118 us -> 0 us
  blocking collectives: 158 us -> 83.5 us
  local copies, waits for them, and re-layouts: 78.8 us -> 11 us
  Pallas kernels: 0 us -> 44.7 us
  waiting for transfers between devices: 51 us -> 20.6 us
  other arithmetic: 21.8 us -> 1.3 us
  between operations: 17.6 us -> 0.16 us
    all_gather x1 -> x0, blocking collectives: 125 us -> none  [body(): lax.all_gather(new_kv, 'ctx', axis=1, tiled=True)]
    dot_general x38 -> x0, matrix products: 118 us -> none  [the longest x19 62.7 us: partial_scores(): jnp.dot(weights, values, precision=HIGHEST, preferred_element_type=jnp.fl...]
    all_to_all x1 -> x3, blocking collectives: 12.3 us -> 83.5 us  [the longest x1 57.6 us: body(): lax.all_to_all(parts, 'ctx', split_axis=0, concat_axis=0, tiled=True, axi...]
    all_gather x1 -> x0, waiting for transfers between devices: 44.9 us -> none  [body(): lax.all_gather(queries, 'ctx', axis=0, tiled=True)]
    pallas_call x0 -> x3, Pallas kernels: none -> 44.7 us  [the longest x1 38 us: attend(): pl.pallas_call(attend_kernel, in_specs=[smem] * 3 + [hbm] * 9 + [vmem] *...]
    gather x11 -> x0, local copies, waits for them, and re-layouts: 34.2 us -> none  [the longest x4 17.8 us: body(): chosen = gathered_q[source_rows, 0].reshape(slots * heads, head_dim)]
    all_to_all x3 -> x0, starting transfers between devices: 23.5 us -> none  [the longest x1 10.1 us: body(): lax.all_to_all(sum_rows.reshape(n_ctx, tok_dev, width), 'ctx', split_axis...]
    ppermute x0 -> x15, waiting for transfers between devices: none -> 20.6 us  [send(): return lax.ppermute(x, 'ctx', [(i, target(i)) for i in range(n_ctx)])]
  transfers between devices with their start and end apart: 4 -> 15, of which waited for: 2 -> 7; matrix products, arithmetic and copies ran while one was open for 11% -> 3% of each run, Pallas kernels for 0% -> 3%
where the time goes in v1:
time: 183 us; the launch traced here: 181 us
  blocking collectives  83.5 us (46%)
  Pallas kernels  44.7 us (24%)
  waiting for transfers between devices  20.6 us (11%)
  starting transfers between devices  20.1 us (11%)
  local copies, waits for them, and re-layouts  11 us (6%)
    all_to_all x1, blocking collectives, body(): lax.all_to_all(parts, 'ctx', split_axis=0, concat_axis=0, tiled=True, axi...  57.6 us
    pallas_call x1, Pallas kernels, attend(): pl.pallas_call(attend_kernel, in_specs=[smem] * 3 + [hbm] * 9 + [vmem] *...  38 us
    ppermute x15, waiting for transfers between devices, send(): return lax.ppermute(x, 'ctx', [(i, target(i)) for i in range(n_ctx)])  20.6 us
    ppermute x15, starting transfers between devices, send(): return lax.ppermute(x, 'ctx', [(i, target(i)) for i in range(n_ctx)])  20.1 us
    all_to_all x1, blocking collectives, body(): lax.all_to_all(jnp.broadcast_to(block_plan[None], (n_ctx,) + block_plan.s...  14.7 us
    all_to_all x1, blocking collectives, body(): lax.all_to_all(wide, 'head', split_axis=0, concat_axis=2, tiled=True)  11.2 us
    unnamed x19, local copies, waits for them, and re-layouts  6.61 us
    pallas_call x1, Pallas kernels, prepare(): pl.pallas_call(prepare_kernel, grid=(REQS,), in_specs=[source] * 4, out_s...  5.96 us
  transfers between devices with their start and end apart: 15, of which 7 were waited for; matrix products, arithmetic and copies ran while one was open for 3% of the time, Pallas kernels for 3%

profile of v1, /device:TPU:4, one launch (start us, length us, event | category | flops | bytes accessed | tf_op | source)
XLA Modules:
  0.0 181.3 jit_solution(16317461113733698025)
XLA Ops:
  0.0 0.0 collective-permute-start.13
  0.0 0.5 collective-permute-start.12
  0.5 0.9 dynamic-slice_bitcast_fusion.2
  1.4 0.1 collective-permute-start
  1.5 2.3 %collective-permute-start.1 = (f32[16,8,128]{2,1,0:T(8,128)S(1)}, f32[16,8,128]{2,1,0:T(8,128)S(1)}, u32[]{:S(2)}, u32[]{:S(2)}) collective-permute-start(f32[16,8,128]{2,1,0:T(8,128)S(1)} %get-tuple-element.11), channel_id=1, source_target_pairs={{0,16},{8,24},{16,0},{24,8},{32,48},{40,56},{48,32},{56,40},{64,80... | collective-permute-start | bytes 196616 | tf_op jit(solution)/shard_map/ppermute | solution.py:337
  3.8 1.0 collective-permute-start.2
  4.9 2.4 %collective-permute-done = f32[16,8,128]{2,1,0:T(8,128)S(1)} collective-permute-done((f32[16,8,128]{2,1,0:T(8,128)S(1)}, f32[16,8,128]{2,1,0:T(8,128)S(1)}, u32[]{:S(2)}, u32[]{:S(2)}) %collective-permute-start) | collective-permute-done | bytes 65568 | tf_op jit(solution)/shard_map/ppermute | solution.py:337
  7.3 0.3 collective-permute-done.1
  7.5 1.9 %collective-permute-done.2 = f32[16,8,128]{2,1,0:T(8,128)S(1)} collective-permute-done((f32[16,8,128]{2,1,0:T(8,128)S(1)}, f32[16,8,128]{2,1,0:T(8,128)S(1)}, u32[]{:S(2)}, u32[]{:S(2)}) %collective-permute-start.2) | collective-permute-done | bytes 65568 | tf_op jit(solution)/shard_map/ppermute | solution.py:337
  9.4 5.0 %collective-permute-start.4 = (f32[64,8,128]{2,1,0:T(8,128)S(1)}, f32[64,8,128]{2,1,0:T(8,128)S(1)}, u32[]{:S(2)}, u32[]{:S(2)}) collective-permute-start(f32[64,8,128]{2,1,0:T(8,128)S(1)} %pad_maximum_fusion.refs_0_), channel_id=1, source_target_pairs={{0,224},{8,232},{16,240},{24,248},{32,0},{40,8},{48,16},{56,24},{6... | collective-permute-start | bytes 786440 | tf_op jit(solution)/shard_map/ppermute | solution.py:337
  14.4 0.0 collective-permute-start.3
  14.4 6.0 %collective-permute-done.4.refs_2_ = f32[64,8,128]{2,1,0:T(8,128)S(1)} collective-permute-done((f32[64,8,128]{2,1,0:T(8,128)S(1)}, f32[64,8,128]{2,1,0:T(8,128)S(1)}, u32[]{:S(2)}, u32[]{:S(2)}) %collective-permute-start.4) | collective-permute-done | bytes 262176 | tf_op jit(solution)/shard_map/ppermute | solution.py:337
  20.4 3.7 %collective-permute-start.6 = (f32[64,8,128]{2,1,0:T(8,128)S(1)}, f32[64,8,128]{2,1,0:T(8,128)S(1)}, u32[]{:S(2)}, u32[]{:S(2)}) collective-permute-start(f32[64,8,128]{2,1,0:T(8,128)S(1)} %collective-permute-done.4.refs_2_), channel_id=1, source_target_pairs={{0,224},{8,232},{16,240},{24,248},{32,0},{40,8},{48,16},{56,24},{6... | collective-permute-start | bytes 786440 | tf_op jit(solution)/shard_map/ppermute | solution.py:337
  24.1 0.0 collective-permute-done.3.refs_1_
  24.1 0.0 collective-permute-start.5
  24.1 5.2 %collective-permute-done.6.refs_4_ = f32[64,8,128]{2,1,0:T(8,128)S(1)} collective-permute-done((f32[64,8,128]{2,1,0:T(8,128)S(1)}, f32[64,8,128]{2,1,0:T(8,128)S(1)}, u32[]{:S(2)}, u32[]{:S(2)}) %collective-permute-start.6) | collective-permute-done | bytes 262176 | tf_op jit(solution)/shard_map/ppermute | solution.py:337
  29.3 3.7 %collective-permute-start.8 = (f32[64,8,128]{2,1,0:T(8,128)S(1)}, f32[64,8,128]{2,1,0:T(8,128)S(1)}, u32[]{:S(2)}, u32[]{:S(2)}) collective-permute-start(f32[64,8,128]{2,1,0:T(8,128)S(1)} %collective-permute-done.6.refs_4_), channel_id=1, source_target_pairs={{0,224},{8,232},{16,240},{24,248},{32,0},{40,8},{48,16},{56,24},{6... | collective-permute-start | bytes 786440 | tf_op jit(solution)/shard_map/ppermute | solution.py:337
  33.0 0.0 copy-start.3
  33.0 0.7 copy-done.3
  33.7 0.0 collective-permute-done.5.refs_3_
  33.7 0.0 copy-start.5
  33.7 0.0 collective-permute-start.7
  33.7 3.6 %collective-permute-done.8.refs_6_ = f32[64,8,128]{2,1,0:T(8,128)S(1)} collective-permute-done((f32[64,8,128]{2,1,0:T(8,128)S(1)}, f32[64,8,128]{2,1,0:T(8,128)S(1)}, u32[]{:S(2)}, u32[]{:S(2)}) %collective-permute-start.8) | collective-permute-done | bytes 262176 | tf_op jit(solution)/shard_map/ppermute | solution.py:337
  37.3 0.7 slice.9
  38.0 3.7 %collective-permute-start.10 = (f32[32,8,128]{2,1,0:T(8,128)}, f32[32,8,128]{2,1,0:T(8,128)S(1)}, u32[]{:S(2)}, u32[]{:S(2)}) collective-permute-start(f32[32,8,128]{2,1,0:T(8,128)} %slice.9), channel_id=1, source_target_pairs={{0,224},{8,232},{16,240},{24,248},{32,0},{40,8},{48,16},{56,24},{6... | collective-permute-start | bytes 393224 | tf_op jit(solution)/shard_map/ppermute | solution.py:337
  41.7 0.0 collective-permute-done.7.refs_5_
  41.7 0.0 copy-done.5
  41.7 0.7 slice.8
  42.3 0.0 collective-permute-start.9
  42.4 0.0 collective-permute-start.11
  42.4 0.7 broadcast_in_dim.2
  43.0 14.7 %all_to_all.26 = s32[32,1,4]{2,1,0:T(1,128)S(1)} all-to-all(s32[32,1,4]{2,1,0:T(1,128)S(1)} %broadcast_in_dim.2), channel_id=1, replica_groups=mesh['ctx'=32,'head'=8] {'ctx'}, dimensions={0} | all-to-all | bytes 1024 | tf_op jit(solution)/shard_map/all_to_all | solution.py:355
  57.7 0.6 broadcast.7
  58.3 1.3 reduce.3
  59.5 0.8 reshape.26.plan
  60.4 0.0 collective-permute-done.13
  60.4 0.0 collective-permute-done.12
  60.4 0.0 copy-start
  60.4 1.6 copy-done
  62.0 0.0 copy-start.1
  62.0 1.6 copy-done.1
  63.6 0.0 copy-start.4
  63.6 0.0 copy-start.6
  63.6 0.0 copy-start.7
  63.6 0.0 copy-start.8
  63.6 6.0 %prepare.1 = (bf16[4,2048,384]{2,1,0:T(8,128)(2,1)}, bf16[4,256,2048]{2,1,0:T(8,128)(2,1)S(1)}) custom-call(f32[4,1024,128]{2,1,0:T(8,128)S(1)} %bitcast.30, f32[4,1024,128]{2,1,0:T(8,128)} %bitcast.7.other_k, f32[4,1024,128]{2,1,0:T(8,128)S(1)} %bitcast.32, f32[4,1024,128]{2,1,0:T(8,128)S(1)} %bitcast.33), custom_call_target="tpu_custom_call" | custom-call | flops 10000000 | bytes 16777216 | tf_op jit(solution)/shard_map/prepare/pallas_call | solution.py:55
  69.5 0.0 copy-start.2
  69.5 2.1 %copy-done.2 = bf16[4,256,2048]{2,1,0:T(8,128)(2,1)} copy-done((bf16[4,256,2048]{2,1,0:T(8,128)(2,1)}, bf16[4,256,2048]{2,1,0:T(8,128)(2,1)S(1)}, u32[]{:S(2)}) %copy-start.2) | copy-done | bytes 4194328
  71.6 0.0 collective-permute-done.11.refs_10_
  71.6 0.0 collective-permute-done.10.refs_8_
  71.6 0.0 collective-permute-done.9.refs_7_
  71.6 0.0 copy-done.4
  71.6 0.0 copy-done.6
  71.6 0.0 copy-done.7
  71.6 0.0 copy-done.8
  71.7 38.0 %attend.1 = f32[16,33,8,128]{3,2,1,0:T(8,128)S(1)} custom-call(s32[4]{0:T(128)S(1)} %copy-done.8, s32[128]{0:T(128)S(1)} %reshape.26.plan, s32[1]{0:T(128)} %bitcast.place, f32[64,8,128]{2,1,0:T(8,128)S(1)} %pad_maximum_fusion.refs_0_, f32[64,8,128]{2,1,0:T(8,128)S(1)} %collective-permute-done.3.refs_1_, f32[64,8,128]{2,1,0:T(8,128)S(1)} %collective-permute-done.4.refs_2_, ...), custom_call_target="tpu_custom_call" | custom-call | flops 33999998976 | bytes 14680064 | tf_op jit(solution)/shard_map/attend/pallas_call | solution.py:273
  109.7 57.6 %all_to_all.27.parts = f32[16,33,8,128]{3,2,1,0:T(8,128)S(1)} all-to-all(f32[16,33,8,128]{3,2,1,0:T(8,128)S(1)} %attend.1), channel_id=1, replica_groups={{0,16,32,48,64,80,96,112,128,144,160,176,192,208,224,240},{8,24,40,56,7..., dimensions={0} | all-to-all | bytes 4325376 | tf_op jit(solution)/shard_map/all_to_all | solution.py:375
  167.3 0.7 merge.1
  168.0 0.1 collective-permute-start.14
  168.1 1.2 collective-permute-done.14
  169.4 0.1 reshape.30
  169.5 11.2 %all_to_all.28 = f32[8,2,1,2048]{3,1,2,0:T(2,128)S(1)} all-to-all(f32[8,2,1,2048]{3,1,2,0:T(2,128)S(1)} %bitcast.38), channel_id=1, replica_groups=mesh['ctx'=32,'head'=8] {'head'}, dimensions={0} | all-to-all | bytes 262144 | tf_op jit(solution)/shard_map/all_to_all | solution.py:385
  180.7 0.7 copy.23
  (4 shorter events, 0.1 us)
Async XLA Ops:
  0.0 60.4 %collective-permute-start.13 = (f32[4,1024,1,128]{3,1,0,2:T(8,128)}, f32[4,1024,1,128]{3,1,0,2:T(8,128)S(1)}, u32[]{:S(2)}, u32[]{:S(2)}) collective-permute-start(f32[4,1024,1,128]{3,1,0,2:T(8,128)} %bitcast.31), channel_id=1, source_target_pairs={{0,8},{8,0},{16,24},{24,16},{32,40},{40,32},{48,56},{56,48},{64,72... | collective-permute-start | bytes 6291464 | tf_op jit(solution)/shard_map/ppermute | solution.py:337
  0.0 60.4 %collective-permute-start.12 = (f32[4,1024,1,128]{3,1,0,2:T(8,128)}, f32[4,1024,1,128]{3,1,0,2:T(8,128)}, u32[]{:S(2)}, u32[]{:S(2)}) collective-permute-start(f32[4,1024,1,128]{3,1,0,2:T(8,128)} %bitcast.29), channel_id=1, source_target_pairs={{0,8},{8,0},{16,24},{24,16},{32,40},{40,32},{48,56},{56,48},{64,72... | collective-permute-start | bytes 6291464 | tf_op jit(solution)/shard_map/ppermute | solution.py:337
  1.4 5.9 %collective-permute-start = (f32[16,8,128]{2,1,0:T(8,128)S(1)}, f32[16,8,128]{2,1,0:T(8,128)S(1)}, u32[]{:S(2)}, u32[]{:S(2)}) collective-permute-start(f32[16,8,128]{2,1,0:T(8,128)S(1)} %get-tuple-element.12), channel_id=1, source_target_pairs={{0,8},{8,0},{16,24},{24,16},{32,40},{40,32},{48,56},{56,48},{64,72... | collective-permute-start | bytes 196616 | tf_op jit(solution)/shard_map/ppermute | solution.py:337
  1.5 6.0 %collective-permute-start.1 = (f32[16,8,128]{2,1,0:T(8,128)S(1)}, f32[16,8,128]{2,1,0:T(8,128)S(1)}, u32[]{:S(2)}, u32[]{:S(2)}) collective-permute-start(f32[16,8,128]{2,1,0:T(8,128)S(1)} %get-tuple-element.11), channel_id=1, source_target_pairs={{0,16},{8,24},{16,0},{24,8},{32,48},{40,56},{48,32},{56,40},{64,80... | collective-permute-start | bytes 196616 | tf_op jit(solution)/shard_map/ppermute | solution.py:337
  3.8 5.6 %collective-permute-start.2 = (f32[16,8,128]{2,1,0:T(8,128)S(1)}, f32[16,8,128]{2,1,0:T(8,128)S(1)}, u32[]{:S(2)}, u32[]{:S(2)}) collective-permute-start(f32[16,8,128]{2,1,0:T(8,128)S(1)} %get-tuple-element.12), channel_id=1, source_target_pairs={{0,24},{8,16},{16,8},{24,0},{32,56},{40,48},{48,40},{56,32},{64,88... | collective-permute-start | bytes 196616 | tf_op jit(solution)/shard_map/ppermute | solution.py:337
  9.4 11.0 %collective-permute-start.4 = (f32[64,8,128]{2,1,0:T(8,128)S(1)}, f32[64,8,128]{2,1,0:T(8,128)S(1)}, u32[]{:S(2)}, u32[]{:S(2)}) collective-permute-start(f32[64,8,128]{2,1,0:T(8,128)S(1)} %pad_maximum_fusion.refs_0_), channel_id=1, source_target_pairs={{0,224},{8,232},{16,240},{24,248},{32,0},{40,8},{48,16},{56,24},{6... | collective-permute-start | bytes 786440 | tf_op jit(solution)/shard_map/ppermute | solution.py:337
  14.4 9.7 %collective-permute-start.3 = (f32[64,8,128]{2,1,0:T(8,128)S(1)}, f32[64,8,128]{2,1,0:T(8,128)S(1)}, u32[]{:S(2)}, u32[]{:S(2)}) collective-permute-start(f32[64,8,128]{2,1,0:T(8,128)S(1)} %pad_maximum_fusion.refs_0_), channel_id=1, source_target_pairs={{0,32},{8,40},{16,48},{24,56},{32,64},{40,72},{48,80},{56,88},{64,... | collective-permute-start | bytes 786440 | tf_op jit(solution)/shard_map/ppermute | solution.py:337
  20.4 8.9 %collective-permute-start.6 = (f32[64,8,128]{2,1,0:T(8,128)S(1)}, f32[64,8,128]{2,1,0:T(8,128)S(1)}, u32[]{:S(2)}, u32[]{:S(2)}) collective-permute-start(f32[64,8,128]{2,1,0:T(8,128)S(1)} %collective-permute-done.4.refs_2_), channel_id=1, source_target_pairs={{0,224},{8,232},{16,240},{24,248},{32,0},{40,8},{48,16},{56,24},{6... | collective-permute-start | bytes 786440 | tf_op jit(solution)/shard_map/ppermute | solution.py:337
  24.1 9.6 %collective-permute-start.5 = (f32[64,8,128]{2,1,0:T(8,128)S(1)}, f32[64,8,128]{2,1,0:T(8,128)S(1)}, u32[]{:S(2)}, u32[]{:S(2)}) collective-permute-start(f32[64,8,128]{2,1,0:T(8,128)S(1)} %collective-permute-done.3.refs_1_), channel_id=1, source_target_pairs={{0,32},{8,40},{16,48},{24,56},{32,64},{40,72},{48,80},{56,88},{64,... | collective-permute-start | bytes 786440 | tf_op jit(solution)/shard_map/ppermute | solution.py:337
  29.3 8.0 %collective-permute-start.8 = (f32[64,8,128]{2,1,0:T(8,128)S(1)}, f32[64,8,128]{2,1,0:T(8,128)S(1)}, u32[]{:S(2)}, u32[]{:S(2)}) collective-permute-start(f32[64,8,128]{2,1,0:T(8,128)S(1)} %collective-permute-done.6.refs_4_), channel_id=1, source_target_pairs={{0,224},{8,232},{16,240},{24,248},{32,0},{40,8},{48,16},{56,24},{6... | collective-permute-start | bytes 786440 | tf_op jit(solution)/shard_map/ppermute | solution.py:337
  33.0 0.7 copy-start.3
  33.7 7.9 %copy-start.5 = (f32[64,8,128]{2,1,0:T(8,128)}, f32[64,8,128]{2,1,0:T(8,128)S(1)}, u32[]{:S(2)}) copy-start(f32[64,8,128]{2,1,0:T(8,128)S(1)} %collective-permute-done.5.refs_3_) | copy-start | bytes 786436
  33.7 7.9 %collective-permute-start.7 = (f32[64,8,128]{2,1,0:T(8,128)S(1)}, f32[64,8,128]{2,1,0:T(8,128)S(1)}, u32[]{:S(2)}, u32[]{:S(2)}) collective-permute-start(f32[64,8,128]{2,1,0:T(8,128)S(1)} %collective-permute-done.5.refs_3_), channel_id=1, source_target_pairs={{0,32},{8,40},{16,48},{24,56},{32,64},{40,72},{48,80},{56,88},{64,... | collective-permute-start | bytes 786440 | tf_op jit(solution)/shard_map/ppermute | solution.py:337
  38.0 33.6 %collective-permute-start.10 = (f32[32,8,128]{2,1,0:T(8,128)}, f32[32,8,128]{2,1,0:T(8,128)S(1)}, u32[]{:S(2)}, u32[]{:S(2)}) collective-permute-start(f32[32,8,128]{2,1,0:T(8,128)} %slice.9), channel_id=1, source_target_pairs={{0,224},{8,232},{16,240},{24,248},{32,0},{40,8},{48,16},{56,24},{6... | collective-permute-start | bytes 393224 | tf_op jit(solution)/shard_map/ppermute | solution.py:337
  42.3 29.3 %collective-permute-start.9 = (f32[32,8,128]{2,1,0:T(8,128)}, f32[32,8,128]{2,1,0:T(8,128)}, u32[]{:S(2)}, u32[]{:S(2)}) collective-permute-start(f32[32,8,128]{2,1,0:T(8,128)} %slice.8), channel_id=1, source_target_pairs={{0,32},{8,40},{16,48},{24,56},{32,64},{40,72},{48,80},{56,88},{64,... | collective-permute-start | bytes 393224 | tf_op jit(solution)/shard_map/ppermute | solution.py:337
  42.4 29.3 %collective-permute-start.11 = (f32[2,16,128]{2,1,0:T(8,128)}, f32[2,16,128]{2,1,0:T(8,128)}, u32[]{:S(2)}, u32[]{:S(2)}) collective-permute-start(f32[2,16,128]{2,1,0:T(8,128)} %bitcast.36), channel_id=1, source_target_pairs={{0,8},{8,0},{16,24},{24,16},{32,40},{40,32},{48,56},{56,48},{64,72... | collective-permute-start | bytes 49160 | tf_op jit(solution)/shard_map/ppermute | solution.py:337
  60.4 1.6 copy-start
  62.0 1.6 copy-start.1
  63.6 8.0 %copy-start.4 = (f32[64,8,128]{2,1,0:T(8,128)S(1)}, f32[64,8,128]{2,1,0:T(8,128)}, u32[]{:S(2)}) copy-start(f32[64,8,128]{2,1,0:T(8,128)} %copy-done.3) | copy-start | bytes 786436
  63.6 8.1 %copy-start.6 = (f32[64,8,128]{2,1,0:T(8,128)S(1)}, f32[64,8,128]{2,1,0:T(8,128)}, u32[]{:S(2)}) copy-start(f32[64,8,128]{2,1,0:T(8,128)} %copy-done.5) | copy-start | bytes 786436
  63.6 8.1 %copy-start.7 = (f32[2,16,1,128]{3,2,1,0:T(1,128)S(1)}, f32[2,16,1,128]{3,2,1,0:T(1,128)}, u32[]{:S(2)}) copy-start(f32[2,16,1,128]{3,2,1,0:T(1,128)} %param.7) | copy-start | bytes 49156
  63.6 8.1 %copy-start.8 = (s32[4]{0:T(128)S(1)}, s32[4]{0:T(128)}, u32[]{:S(2)}) copy-start(s32[4]{0:T(128)} %lengths.1) | copy-start | bytes 52
  69.5 2.1 %copy-start.2 = (bf16[4,256,2048]{2,1,0:T(8,128)(2,1)}, bf16[4,256,2048]{2,1,0:T(8,128)(2,1)S(1)}, u32[]{:S(2)}) copy-start(bf16[4,256,2048]{2,1,0:T(8,128)(2,1)S(1)} %get-tuple-element.8.refs_12_) | copy-start | bytes 12582916
  168.0 1.3 collective-permute-start.14
